TPU v7x, 256 devices: a whole 4x4x8 slice. The times are simulated.
256 devices in a mesh: lon: 32 (over y, x, core), lat: 8 (over z).
Axes of the slice: x: 4, y: 4, z: 8, core: 2. Of those that a mesh axis runs over, the one named last changes fastest.
Arguments:
- state: bfloat16 [2, 128, 4096, 256], P(None, 'lat', 'lon'), may hold values from -6 to 6
- ocean_mask: int32 [2, 128, 4096], P(None, 'lat', 'lon'), may hold values from 0 to 1, as said below
- norm_gain: float32 [256], replicated, may hold values from 0.25 to 1.75
- w_qkv: bfloat16 [256, 768], replicated
- w_out: bfloat16 [256, 256], replicated, may hold values from -0.375 to 0.375
Outputs:
- updated: bfloat16 [2, 128, 4096, 256], P(None, 'lat', 'lon')
Inputs may be any that keep to these rules, and one draw needn't show every extreme that they name: `ocean_mask`: 1 marks ocean; a cell that is ocean at a level is ocean at every lower-index level.
All inputs are finite; a program needn't handle non-finite values.
Results may differ from a plain program's by a relative error of at most 0.0028.
The roundings to bfloat16 on the way count: a program that leaves them out, or rounds other values in their place, can miss the bound.
Values may be sent and summed in bfloat16 or wider, within the bound.
No kernel may reach another device: no remote copies, remote signals or barrier semaphores. Data moves between devices by JAX's collectives and lax.ppermute only.
A program may use at most 64 MiB of HBM per device.

v0:
```python
import jax
import jax.numpy as jnp
from jax import lax
from jax.sharding import PartitionSpec as P

C = 256
HEADS = 8
W = 16
SHIFT = 8


def from_behind(x, axis, by):
    size = lax.axis_size(axis)
    pairs = [(i, i + by) for i in range(size) if 0 <= i + by < size]
    return lax.ppermute(x, axis, pairs)


def partner(x, axis, stride):
    return lax.ppermute(x, axis, [(i, i ^ 1 << stride) for i in range(lax.axis_size(axis))])


def shifted_2(x, axis, by):
    size = lax.axis_size(axis)
    return lax.ppermute(x, axis, [(i, (i + by) % size) for i in range(size)])


def window_update(tokens, ocean, norm_gain, w_qkv, w_out):
    values_f = tokens.astype(jnp.float32)
    average = jnp.mean(values_f, axis=1, keepdims=True)
    spread_sq = jnp.mean((values_f - average) ** 2, axis=1, keepdims=True)
    normed = ((values_f - average) * lax.rsqrt(spread_sq + 1e-05) * norm_gain).astype(jnp.bfloat16)
    projected = jnp.dot(normed, w_qkv, preferred_element_type=jnp.float32)
    head_size = C // HEADS
    queries = (projected[:, :C] * (1.0 / head_size**0.5)).astype(jnp.bfloat16)
    keys_bf = projected[:, C : 2 * C].astype(jnp.bfloat16)
    values_bf = projected[:, 2 * C :].astype(jnp.bfloat16)
    count = tokens.shape[0]
    queries = queries.reshape(count, HEADS, head_size).transpose(1, 0, 2)
    keys_bf = keys_bf.reshape(count, HEADS, head_size).transpose(1, 0, 2)
    values_bf = values_bf.reshape(count, HEADS, head_size).transpose(1, 0, 2)
    allowed = ocean[None, :] > 0

    def one_head(pieces):
        query_h, key_h, value_h = pieces
        scores = jnp.dot(query_h, key_h.T, preferred_element_type=jnp.float32)
        top_score = jnp.max(jnp.where(allowed, scores, -1e30), axis=1, keepdims=True)
        weights = jnp.where(allowed, jnp.exp(jnp.where(allowed, scores - top_score, 0.0)), 0.0)
        total = jnp.sum(weights, axis=1) + (1.0 - ocean)
        mixed = jnp.dot(weights.astype(jnp.bfloat16), value_h, preferred_element_type=jnp.float32)
        return mixed / total[:, None]

    mixed = lax.map(one_head, (queries, keys_bf, values_bf))
    mixed = mixed.transpose(1, 0, 2).reshape(count, C).astype(jnp.bfloat16)
    delta = jnp.dot(mixed, w_out, preferred_element_type=jnp.float32) * ocean[:, None]
    return delta.astype(jnp.bfloat16)


def to_windows(grid):
    rest = grid.shape[3:]
    levels_n, rows_n, cols_n = (grid.shape[0], grid.shape[1], grid.shape[2])
    shaped = grid.reshape((levels_n, rows_n // W, W, cols_n // W, W) + rest)
    order = (1, 3, 2, 4, 0) + tuple(range(5, 5 + len(rest)))
    return shaped.transpose(order).reshape((rows_n // W * (cols_n // W), W * W * levels_n) + rest)


def from_windows(blocks, levels_n, rows_n, cols_n):
    width = blocks.shape[-1]
    shaped = blocks.reshape(rows_n // W, cols_n // W, W, W, levels_n, width)
    return shaped.transpose(4, 0, 2, 1, 3, 5).reshape(levels_n, rows_n, cols_n, width)


def shards(state, ocean_mask, norm_gain, w_qkv, w_out):
    rows_n = state.shape[1]
    cols_n = state.shape[2]
    mask_bf = ocean_mask.astype(jnp.bfloat16)
    above_state, above_mask = from_behind((state[:, :SHIFT], mask_bf[:, :SHIFT]), "lat", -1)
    fold_state = state[:, rows_n - SHIFT :][:, ::-1, ::-1]
    fold_mask = mask_bf[:, rows_n - SHIFT :][:, ::-1, ::-1]
    bit_list = list(range(lax.axis_size("lon").bit_length() - 1))
    for bit_number in bit_list:
        fold_state, fold_mask = partner((fold_state, fold_mask), "lon", bit_number)
    is_top = lax.axis_index("lat") == lax.axis_size("lat") - 1
    upper_state = jnp.where(is_top, fold_state, above_state)
    upper_mask = jnp.where(is_top, fold_mask, above_mask)
    row_state = jnp.concatenate([state[:, SHIFT:], upper_state], axis=1)
    row_mask = jnp.concatenate([mask_bf[:, SHIFT:], upper_mask], axis=1)
    right_state, right_mask = shifted_2(
        (row_state[:, :, :SHIFT], row_mask[:, :, :SHIFT]), "lon", -1
    )
    shifted = jnp.concatenate([row_state[:, :, SHIFT:], right_state], axis=2)
    shifted_mask = jnp.concatenate([row_mask[:, :, SHIFT:], right_mask], axis=2).astype(jnp.float32)
    win_state = to_windows(shifted)
    win_mask = to_windows(shifted_mask)

    def per_window(pieces):
        tokens, ocean = pieces
        return window_update(tokens, ocean, norm_gain, w_qkv, w_out)

    deltas = lax.map(per_window, (win_state, win_mask))
    delta = from_windows(deltas, state.shape[0], rows_n, cols_n)
    left_part = shifted_2(delta[:, :, cols_n - SHIFT :], "lon", 1)
    col_aligned = jnp.concatenate([left_part, delta[:, :, : cols_n - SHIFT]], axis=2)
    below_part = from_behind(col_aligned[:, rows_n - SHIFT :], "lat", 1)
    placed = jnp.concatenate([below_part, col_aligned[:, : rows_n - SHIFT]], axis=1)
    return (state.astype(jnp.float32) + placed.astype(jnp.float32)).astype(jnp.bfloat16)


def solution(mesh):
    in_specs = (P(None, "lat", "lon", None), P(None, "lat", "lon"), P(), P(), P())
    out_specs = P(None, "lat", "lon", None)
    return jax.shard_map(shards, mesh=mesh, in_specs=in_specs, out_specs=out_specs, check_vma=False)
```

profile of v0, /device:TPU:224, one launch (start us, length us, event | category | flops | bytes accessed | tf_op | source)
XLA Modules:
  0.0 312.7 jit_solution(6131436391742085729)
XLA Ops:
  0.0 2.7 fusion.40
  2.7 1.3 rev.6
  4.1 2.6 collective-permute-done
  6.7 1.5 collective-permute-start.1
  8.2 23.7 %collective-permute-done.1 = bf16[2,8,128,256]{3,2,1,0:T(8,128)(2,1)S(1)} collective-permute-done((bf16[2,8,128,256]{3,2,1,0:T(8,128)(2,1)S(1)}, bf16[2,8,128,256]{3,2,1,0:T(8,128)(2,1)S(1)}, u32[]{:S(2)}, u32[]{:S(2)}) %collective-permute-start.1) | collective-permute-done | bytes 1048608 | tf_op jit(solution)/shard_map/ppermute | solution.py:19
  31.9 3.0 collective-permute-start.2
  35.0 22.9 %collective-permute-done.2 = bf16[2,8,128,256]{3,2,1,0:T(8,128)(2,1)S(1)} collective-permute-done((bf16[2,8,128,256]{3,2,1,0:T(8,128)(2,1)S(1)}, bf16[2,8,128,256]{3,2,1,0:T(8,128)(2,1)S(1)}, u32[]{:S(2)}, u32[]{:S(2)}) %collective-permute-start.2) | collective-permute-done | bytes 1048608 | tf_op jit(solution)/shard_map/ppermute | solution.py:19
  57.8 1.6 collective-permute-start.3
  59.4 3.0 collective-permute-start.5
  62.4 19.0 %collective-permute-done.3 = bf16[2,8,128,256]{3,2,1,0:T(8,128)(2,1)} collective-permute-done((bf16[2,8,128,256]{3,2,1,0:T(8,128)(2,1)S(1)}, bf16[2,8,128,256]{3,2,1,0:T(8,128)(2,1)}, u32[]{:S(2)}, u32[]{:S(2)}) %collective-permute-start.3) | collective-permute-done | bytes 1048608 | tf_op jit(solution)/shard_map/ppermute | solution.py:19
  81.4 3.2 %collective-permute-start.4 = (bf16[2,8,128,256]{3,2,1,0:T(8,128)(2,1)}, bf16[2,8,128,256]{3,2,1,0:T(8,128)(2,1)S(1)}, u32[]{:S(2)}, u32[]{:S(2)}) collective-permute-start(bf16[2,8,128,256]{3,2,1,0:T(8,128)(2,1)} %collective-permute-done.3), channel_id=1, source_target_pairs={{0,128},{8,136},{16,144},{24,152},{32,160},{40,168},{48,176},{56,1... | collective-permute-start | bytes 3145736 | tf_op jit(solution)/shard_map/ppermute | solution.py:19
  84.7 1.2 collective-permute-done.7
  85.9 1.5 collective-permute-start.8
  87.4 2.1 collective-permute-done.8
  89.5 3.0 collective-permute-start.9
  92.5 2.1 collective-permute-done.9
  94.6 1.2 collective-permute-start.10
  95.8 2.9 collective-permute-start.12
  98.7 7.4 %collective-permute-done.10 = bf16[2,8,128]{2,1,0:T(8,128)(2,1)S(1)} collective-permute-done((bf16[2,8,128]{2,1,0:T(8,128)(2,1)S(1)}, bf16[2,8,128]{2,1,0:T(8,128)(2,1)S(1)}, u32[]{:S(2)}, u32[]{:S(2)}) %collective-permute-start.10) | collective-permute-done | bytes 4128 | tf_op jit(solution)/shard_map/ppermute | solution.py:19
  106.1 1.8 collective-permute-start.11
  107.9 3.3 %collective-permute-done.11 = bf16[2,8,128]{2,1,0:T(8,128)(2,1)S(1)} collective-permute-done((bf16[2,8,128]{2,1,0:T(8,128)(2,1)S(1)}, bf16[2,8,128]{2,1,0:T(8,128)(2,1)S(1)}, u32[]{:S(2)}, u32[]{:S(2)}) %collective-permute-start.11) | collective-permute-done | bytes 4128 | tf_op jit(solution)/shard_map/ppermute | solution.py:19
  111.4 1.3 collective-permute-done.13
  113.3 5.3 %collective-permute-start.6 = (bf16[2,16,8,256]{3,2,1,0:T(8,128)(2,1)S(1)}, bf16[2,16,8,256]{3,2,1,0:T(8,128)(2,1)S(1)}, u32[]{:S(2)}, u32[]{:S(2)}) collective-permute-start(bf16[2,16,8,256]{3,2,1,0:T(8,128)(2,1)S(1)} %pad_maximum_fusion.2), channel_id=1, source_target_pairs={{0,248},{8,0},{16,8},{24,16},{32,24},{40,32},{48,40},{56,48},{64,5... | collective-permute-start | bytes 393224 | tf_op jit(solution)/shard_map/ppermute | solution.py:24
  118.7 2.3 collective-permute-done.6
  121.4 4.6 %copy.26 = bf16[2,1,16,8,16,256]{5,0,4,2,3,1:T(2,128)(2,1)} copy(bf16[2,1,16,8,16,256]{5,4,3,2,0,1:T(8,128)(2,1)S(1)} %bitcast.101) | data formatting | bytes 4194304 | tf_op jit(solution)/shard_map/reshape | solution.py:61
  125.9 2.8 reshape.66
  128.8 150.2 %while.21 = (s32[]{:T(128)}, bf16[8,512,256]{2,1,0:T(8,128)(2,1)}, bf16[8,512,256]{2,1,0:T(8,128)(2,1)S(1)}, f32[256]{0:T(256)S(1)}, bf16[256,768]{1,0:T(8,128)(...) while((s32[]{:T(128)}, bf16[8,512,256]{2,1,0:T(8,128)(2,1)}, ...), condition=%wide.region_7.8_spmd, body=%wide.region_0.7_spmd.sunk | while | flops 306988032 | bytes 27737440 | solution.py:99
  130.1 1.4 fusion.61
  132.1 13.5 %while.22 = (s32[]{:T(128)}, bf16[8,512,32]{1,2,0:T(8,128)(2,1)}, pred[1,512]{1,0:T(4,128)(4,1)S(1)}, bf16[8,512,32]{1,2,0:T(8,128)(2,1)S(1)}, bf16[8,512,32]{1,...) while((s32[]{:T(128)}, bf16[8,512,32]{1,2,0:T(8,128)(2,1)}, ...), condition=%wide.region_6.6_spmd, body=%wide.region_3.5_spmd.sunk | while | flops 36192256 | bytes 3330654 | solution.py:52
  141.3 1.0 fusion.68
  145.6 1.9 fusion.64
  148.9 1.4 fusion.61
  150.9 13.5 %while.22 = (s32[]{:T(128)}, bf16[8,512,32]{1,2,0:T(8,128)(2,1)}, pred[1,512]{1,0:T(4,128)(4,1)S(1)}, bf16[8,512,32]{1,2,0:T(8,128)(2,1)S(1)}, bf16[8,512,32]{1,...) while((s32[]{:T(128)}, bf16[8,512,32]{1,2,0:T(8,128)(2,1)}, ...), condition=%wide.region_6.6_spmd, body=%wide.region_3.5_spmd.sunk | while | flops 36192256 | bytes 3330654 | solution.py:52
  160.1 1.0 fusion.68
  164.4 1.9 fusion.64
  167.7 1.4 fusion.61
  169.7 13.5 %while.22 = (s32[]{:T(128)}, bf16[8,512,32]{1,2,0:T(8,128)(2,1)}, pred[1,512]{1,0:T(4,128)(4,1)S(1)}, bf16[8,512,32]{1,2,0:T(8,128)(2,1)S(1)}, bf16[8,512,32]{1,...) while((s32[]{:T(128)}, bf16[8,512,32]{1,2,0:T(8,128)(2,1)}, ...), condition=%wide.region_6.6_spmd, body=%wide.region_3.5_spmd.sunk | while | flops 36192256 | bytes 3330654 | solution.py:52
  178.8 1.0 fusion.68
  183.2 1.9 fusion.64
  186.5 1.4 fusion.61
  188.5 13.5 %while.22 = (s32[]{:T(128)}, bf16[8,512,32]{1,2,0:T(8,128)(2,1)}, pred[1,512]{1,0:T(4,128)(4,1)S(1)}, bf16[8,512,32]{1,2,0:T(8,128)(2,1)S(1)}, bf16[8,512,32]{1,...) while((s32[]{:T(128)}, bf16[8,512,32]{1,2,0:T(8,128)(2,1)}, ...), condition=%wide.region_6.6_spmd, body=%wide.region_3.5_spmd.sunk | while | flops 36192256 | bytes 3330654 | solution.py:52
  197.6 1.0 fusion.68
  202.0 1.9 fusion.64
  205.2 1.4 fusion.61
  207.2 13.5 %while.22 = (s32[]{:T(128)}, bf16[8,512,32]{1,2,0:T(8,128)(2,1)}, pred[1,512]{1,0:T(4,128)(4,1)S(1)}, bf16[8,512,32]{1,2,0:T(8,128)(2,1)S(1)}, bf16[8,512,32]{1,...) while((s32[]{:T(128)}, bf16[8,512,32]{1,2,0:T(8,128)(2,1)}, ...), condition=%wide.region_6.6_spmd, body=%wide.region_3.5_spmd.sunk | while | flops 36192256 | bytes 3330654 | solution.py:52
  216.4 1.0 fusion.68
  220.8 1.9 fusion.64
  224.0 1.4 fusion.61
  226.0 13.5 %while.22 = (s32[]{:T(128)}, bf16[8,512,32]{1,2,0:T(8,128)(2,1)}, pred[1,512]{1,0:T(4,128)(4,1)S(1)}, bf16[8,512,32]{1,2,0:T(8,128)(2,1)S(1)}, bf16[8,512,32]{1,...) while((s32[]{:T(128)}, bf16[8,512,32]{1,2,0:T(8,128)(2,1)}, ...), condition=%wide.region_6.6_spmd, body=%wide.region_3.5_spmd.sunk | while | flops 36192256 | bytes 3330654 | solution.py:52
  235.2 1.0 fusion.68
  239.5 1.9 fusion.64
  242.8 1.4 fusion.61
  244.8 13.5 %while.22 = (s32[]{:T(128)}, bf16[8,512,32]{1,2,0:T(8,128)(2,1)}, pred[1,512]{1,0:T(4,128)(4,1)S(1)}, bf16[8,512,32]{1,2,0:T(8,128)(2,1)S(1)}, bf16[8,512,32]{1,...) while((s32[]{:T(128)}, bf16[8,512,32]{1,2,0:T(8,128)(2,1)}, ...), condition=%wide.region_6.6_spmd, body=%wide.region_3.5_spmd.sunk | while | flops 36192256 | bytes 3330654 | solution.py:52
  254.0 1.0 fusion.68
  258.3 1.9 fusion.64
  261.6 1.4 fusion.61
  263.6 13.5 %while.22 = (s32[]{:T(128)}, bf16[8,512,32]{1,2,0:T(8,128)(2,1)}, pred[1,512]{1,0:T(4,128)(4,1)S(1)}, bf16[8,512,32]{1,2,0:T(8,128)(2,1)S(1)}, bf16[8,512,32]{1,...) while((s32[]{:T(128)}, bf16[8,512,32]{1,2,0:T(8,128)(2,1)}, ...), condition=%wide.region_6.6_spmd, body=%wide.region_3.5_spmd.sunk | while | flops 36192256 | bytes 3330654 | solution.py:52
  272.7 1.0 fusion.68
  277.1 1.9 fusion.64
  279.0 2.7 reshape.69
  282.5 7.7 %collective-permute-done.14 = bf16[2,16,8,256]{3,2,1,0:T(8,128)(2,1)S(1)} collective-permute-done((bf16[2,16,8,256]{3,2,1,0:T(8,128)(2,1)S(1)}, bf16[2,16,8,256]{3,2,1,0:T(8,128)(2,1)S(1)}, u32[]{:S(2)}, u32[]{:S(2)}) %collective-permute-start.14) | collective-permute-done | bytes 131104 | tf_op jit(solution)/shard_map/ppermute | solution.py:24
  290.3 1.3 collective-permute-start.15
  291.6 19.2 %collective-permute-done.15 = bf16[2,8,128,256]{3,2,1,0:T(8,128)(2,1)S(1)} collective-permute-done((bf16[2,8,128,256]{3,2,1,0:T(8,128)(2,1)S(1)}, bf16[2,8,128,256]{3,2,1,0:T(8,128)(2,1)S(1)}, u32[]{:S(2)}, u32[]{:S(2)}) %collective-permute-start.15) | collective-permute-done | bytes 1048608 | tf_op jit(solution)/shard_map/ppermute | solution.py:15
  310.7 2.0 add_convert_fusion
  (468 shorter events, 116.2 us)
Async XLA Ops:
  2.7 81.8 %copy-start.5 = (s32[2,16,128]{2,1,0:T(8,128)S(1)}, s32[2,16,128]{2,1,0:T(8,128)}, u32[]{:S(2)}) copy-start(s32[2,16,128]{2,1,0:T(8,128)} %param.10) | copy-start | bytes 49156
  4.0 2.7 collective-permute-start
  6.7 25.2 %collective-permute-start.1 = (bf16[2,8,128,256]{3,2,1,0:T(8,128)(2,1)S(1)}, bf16[2,8,128,256]{3,2,1,0:T(8,128)(2,1)S(1)}, u32[]{:S(2)}, u32[]{:S(2)}) collective-permute-start(bf16[2,8,128,256]{3,2,1,0:T(8,128)(2,1)S(1)} %collective-permute-done), channel_id=1, source_target_pairs={{0,16},{8,24},{16,0},{24,8},{32,48},{40,56},{48,32},{56,40},{64,80... | collective-permute-start | bytes 3145736 | tf_op jit(solution)/shard_map/ppermute | solution.py:19
  31.9 25.9 %collective-permute-start.2 = (bf16[2,8,128,256]{3,2,1,0:T(8,128)(2,1)S(1)}, bf16[2,8,128,256]{3,2,1,0:T(8,128)(2,1)S(1)}, u32[]{:S(2)}, u32[]{:S(2)}) collective-permute-start(bf16[2,8,128,256]{3,2,1,0:T(8,128)(2,1)S(1)} %collective-permute-done.1), channel_id=1, source_target_pairs={{0,32},{8,40},{16,48},{24,56},{32,0},{40,8},{48,16},{56,24},{64,96... | collective-permute-start | bytes 3145736 | tf_op jit(solution)/shard_map/ppermute | solution.py:19
  57.8 23.6 %collective-permute-start.3 = (bf16[2,8,128,256]{3,2,1,0:T(8,128)(2,1)S(1)}, bf16[2,8,128,256]{3,2,1,0:T(8,128)(2,1)}, u32[]{:S(2)}, u32[]{:S(2)}) collective-permute-start(bf16[2,8,128,256]{3,2,1,0:T(8,128)(2,1)S(1)} %collective-permute-done.2), channel_id=1, source_target_pairs={{0,64},{8,72},{16,80},{24,88},{32,96},{40,104},{48,112},{56,120},{... | collective-permute-start | bytes 3145736 | tf_op jit(solution)/shard_map/ppermute | solution.py:19
  59.4 53.7 %collective-permute-start.5 = (bf16[2,8,128,256]{3,2,1,0:T(8,128)(2,1)}, bf16[2,8,128,256]{3,2,1,0:T(8,128)(2,1)S(1)}, u32[]{:S(2)}, u32[]{:S(2)}) collective-permute-start(bf16[2,8,128,256]{3,2,1,0:T(8,128)(2,1)} %get-tuple-element.130), channel_id=1, source_target_pairs={{1,0},{2,1},{3,2},{4,3},{5,4},{6,5},{7,6},{9,8},{10,9},{11,10},{12... | collective-permute-start | bytes 3145736 | tf_op jit(solution)/shard_map/ppermute | solution.py:15
  81.4 31.7 %collective-permute-start.4 = (bf16[2,8,128,256]{3,2,1,0:T(8,128)(2,1)}, bf16[2,8,128,256]{3,2,1,0:T(8,128)(2,1)S(1)}, u32[]{:S(2)}, u32[]{:S(2)}) collective-permute-start(bf16[2,8,128,256]{3,2,1,0:T(8,128)(2,1)} %collective-permute-done.3), channel_id=1, source_target_pairs={{0,128},{8,136},{16,144},{24,152},{32,160},{40,168},{48,176},{56,1... | collective-permute-start | bytes 3145736 | tf_op jit(solution)/shard_map/ppermute | solution.py:19
  84.7 1.2 collective-permute-start.7
  85.9 3.6 %collective-permute-start.8 = (bf16[2,8,128]{2,1,0:T(8,128)(2,1)S(1)}, bf16[2,8,128]{2,1,0:T(8,128)(2,1)S(1)}, u32[]{:S(2)}, u32[]{:S(2)}) collective-permute-start(bf16[2,8,128]{2,1,0:T(8,128)(2,1)S(1)} %collective-permute-done.7), channel_id=1, source_target_pairs={{0,16},{8,24},{16,0},{24,8},{32,48},{40,56},{48,32},{56,40},{64,80... | collective-permute-start | bytes 12296 | tf_op jit(solution)/shard_map/ppermute | solution.py:19
  89.5 5.1 %collective-permute-start.9 = (bf16[2,8,128]{2,1,0:T(8,128)(2,1)S(1)}, bf16[2,8,128]{2,1,0:T(8,128)(2,1)S(1)}, u32[]{:S(2)}, u32[]{:S(2)}) collective-permute-start(bf16[2,8,128]{2,1,0:T(8,128)(2,1)S(1)} %collective-permute-done.8), channel_id=1, source_target_pairs={{0,32},{8,40},{16,48},{24,56},{32,0},{40,8},{48,16},{56,24},{64,96... | collective-permute-start | bytes 12296 | tf_op jit(solution)/shard_map/ppermute | solution.py:19
  94.6 11.5 %collective-permute-start.10 = (bf16[2,8,128]{2,1,0:T(8,128)(2,1)S(1)}, bf16[2,8,128]{2,1,0:T(8,128)(2,1)S(1)}, u32[]{:S(2)}, u32[]{:S(2)}) collective-permute-start(bf16[2,8,128]{2,1,0:T(8,128)(2,1)S(1)} %collective-permute-done.9), channel_id=1, source_target_pairs={{0,64},{8,72},{16,80},{24,88},{32,96},{40,104},{48,112},{56,120},{... | collective-permute-start | bytes 12296 | tf_op jit(solution)/shard_map/ppermute | solution.py:19
  95.8 12.1 %collective-permute-start.12 = (bf16[2,8,128]{2,1,0:T(8,128)(2,1)S(1)}, bf16[2,8,128]{2,1,0:T(8,128)(2,1)S(1)}, u32[]{:S(2)}, u32[]{:S(2)}) collective-permute-start(bf16[2,8,128]{2,1,0:T(8,128)(2,1)S(1)} %get-tuple-element.132), channel_id=1, source_target_pairs={{1,0},{2,1},{3,2},{4,3},{5,4},{6,5},{7,6},{9,8},{10,9},{11,10},{12... | collective-permute-start | bytes 12296 | tf_op jit(solution)/shard_map/ppermute | solution.py:15
  106.1 5.1 %collective-permute-start.11 = (bf16[2,8,128]{2,1,0:T(8,128)(2,1)S(1)}, bf16[2,8,128]{2,1,0:T(8,128)(2,1)S(1)}, u32[]{:S(2)}, u32[]{:S(2)}) collective-permute-start(bf16[2,8,128]{2,1,0:T(8,128)(2,1)S(1)} %collective-permute-done.10), channel_id=1, source_target_pairs={{0,128},{8,136},{16,144},{24,152},{32,160},{40,168},{48,176},{56,1... | collective-permute-start | bytes 12296 | tf_op jit(solution)/shard_map/ppermute | solution.py:19
  111.2 1.4 collective-permute-start.13
  113.3 7.8 %collective-permute-start.6 = (bf16[2,16,8,256]{3,2,1,0:T(8,128)(2,1)S(1)}, bf16[2,16,8,256]{3,2,1,0:T(8,128)(2,1)S(1)}, u32[]{:S(2)}, u32[]{:S(2)}) collective-permute-start(bf16[2,16,8,256]{3,2,1,0:T(8,128)(2,1)S(1)} %pad_maximum_fusion.2), channel_id=1, source_target_pairs={{0,248},{8,0},{16,8},{24,16},{32,24},{40,32},{48,40},{56,48},{64,5... | collective-permute-start | bytes 393224 | tf_op jit(solution)/shard_map/ppermute | solution.py:24
  125.9 2.8 copy-start.2
  125.9 2.8 copy-start.4
  125.9 2.8 copy-start.6
  128.8 1.3 copy-start
  132.1 15.5 %copy-start.1 = (bf16[8,512,256]{2,1,0:T(8,128)(2,1)S(1)}, bf16[8,512,256]{2,1,0:T(8,128)(2,1)}, u32[]{:S(2)}) copy-start(bf16[8,512,256]{2,1,0:T(8,128)(2,1)} %copy-done) | copy-start | bytes 6291460 | tf_op jit(solution)/shard_map/while
  147.6 1.3 copy-start
  150.9 15.5 %copy-start.1 = (bf16[8,512,256]{2,1,0:T(8,128)(2,1)S(1)}, bf16[8,512,256]{2,1,0:T(8,128)(2,1)}, u32[]{:S(2)}) copy-start(bf16[8,512,256]{2,1,0:T(8,128)(2,1)} %copy-done) | copy-start | bytes 6291460 | tf_op jit(solution)/shard_map/while
  166.4 1.3 copy-start
  169.7 15.5 %copy-start.1 = (bf16[8,512,256]{2,1,0:T(8,128)(2,1)S(1)}, bf16[8,512,256]{2,1,0:T(8,128)(2,1)}, u32[]{:S(2)}) copy-start(bf16[8,512,256]{2,1,0:T(8,128)(2,1)} %copy-done) | copy-start | bytes 6291460 | tf_op jit(solution)/shard_map/while
  185.1 1.3 copy-start
  188.5 15.5 %copy-start.1 = (bf16[8,512,256]{2,1,0:T(8,128)(2,1)S(1)}, bf16[8,512,256]{2,1,0:T(8,128)(2,1)}, u32[]{:S(2)}) copy-start(bf16[8,512,256]{2,1,0:T(8,128)(2,1)} %copy-done) | copy-start | bytes 6291460 | tf_op jit(solution)/shard_map/while
  203.9 1.3 copy-start
  207.2 15.5 %copy-start.1 = (bf16[8,512,256]{2,1,0:T(8,128)(2,1)S(1)}, bf16[8,512,256]{2,1,0:T(8,128)(2,1)}, u32[]{:S(2)}) copy-start(bf16[8,512,256]{2,1,0:T(8,128)(2,1)} %copy-done) | copy-start | bytes 6291460 | tf_op jit(solution)/shard_map/while
  222.7 1.3 copy-start
  226.0 15.5 %copy-start.1 = (bf16[8,512,256]{2,1,0:T(8,128)(2,1)S(1)}, bf16[8,512,256]{2,1,0:T(8,128)(2,1)}, u32[]{:S(2)}) copy-start(bf16[8,512,256]{2,1,0:T(8,128)(2,1)} %copy-done) | copy-start | bytes 6291460 | tf_op jit(solution)/shard_map/while
  241.5 1.3 copy-start
  244.8 15.5 %copy-start.1 = (bf16[8,512,256]{2,1,0:T(8,128)(2,1)S(1)}, bf16[8,512,256]{2,1,0:T(8,128)(2,1)}, u32[]{:S(2)}) copy-start(bf16[8,512,256]{2,1,0:T(8,128)(2,1)} %copy-done) | copy-start | bytes 6291460 | tf_op jit(solution)/shard_map/while
  260.3 1.3 copy-start
  263.6 15.5 %copy-start.1 = (bf16[8,512,256]{2,1,0:T(8,128)(2,1)S(1)}, bf16[8,512,256]{2,1,0:T(8,128)(2,1)}, u32[]{:S(2)}) copy-start(bf16[8,512,256]{2,1,0:T(8,128)(2,1)} %copy-done) | copy-start | bytes 6291460 | tf_op jit(solution)/shard_map/while
  282.2 7.9 %collective-permute-start.14 = (bf16[2,16,8,256]{3,2,1,0:T(8,128)(2,1)S(1)}, bf16[2,16,8,256]{3,2,1,0:T(8,128)(2,1)S(1)}, u32[]{:S(2)}, u32[]{:S(2)}) collective-permute-start(bf16[2,16,8,256]{3,2,1,0:T(8,128)(2,1)S(1)} %slice.70), channel_id=1, source_target_pairs={{0,8},{8,16},{16,24},{24,32},{32,40},{40,48},{48,56},{56,64},{64,7... | collective-permute-start | bytes 393224 | tf_op jit(solution)/shard_map/ppermute | solution.py:24
  282.5 28.2 %copy-start.3 = (bf16[2,16,128,256]{3,2,1,0:T(8,128)(2,1)S(1)}, bf16[2,16,128,256]{3,2,1,0:T(8,128)(2,1)}, u32[]{:S(2)}) copy-start(bf16[2,16,128,256]{3,2,1,0:T(8,128)(2,1)} %param.9) | copy-start | bytes 6291460
  290.3 20.5 %collective-permute-start.15 = (bf16[2,8,128,256]{3,2,1,0:T(8,128)(2,1)S(1)}, bf16[2,8,128,256]{3,2,1,0:T(8,128)(2,1)S(1)}, u32[]{:S(2)}, u32[]{:S(2)}) collective-permute-start(bf16[2,8,128,256]{3,2,1,0:T(8,128)(2,1)S(1)} %fusion.37), channel_id=1, source_target_pairs={{0,1},{1,2},{2,3},{3,4},{4,5},{5,6},{6,7},{8,9},{9,10},{10,11},{11... | collective-permute-start | bytes 3145736 | tf_op jit(solution)/shard_map/ppermute | solution.py:15
where the time goes:
time: 316 us; the launch traced here: 313 us
  waiting for transfers between devices  115 us (36%)
  matrix products  113 us (36%)
  starting transfers between devices  29.5 us (9%)
  other arithmetic  27.1 us (9%)
  local copies, waits for them, and re-layouts  26.3 us (8%)
    ppermute x10, waiting for transfers between devices, partner(): lax.ppermute(x, axis, [(i, i ^ 1 << stride) for i in range(lax.axis_size(...  84.3 us
    dot_general x64, matrix products, one_head(): jnp.dot(weights.astype(jnp.bfloat16), value_h, preferred_element_type=jnp...  63 us
    dot_general x64, matrix products, one_head(): scores = jnp.dot(query_h, key_h.T, preferred_element_type=jnp.float32)  23.6 us
    ppermute x3, waiting for transfers between devices, from_behind(): return lax.ppermute(x, axis, pairs)  19.2 us
    reduce_sum x64, other arithmetic, one_head(): total = jnp.sum(weights, axis=1) + (1.0 - ocean)  19 us
    ppermute x10, starting transfers between devices, partner(): lax.ppermute(x, axis, [(i, i ^ 1 << stride) for i in range(lax.axis_size(...  16.9 us
    dot_general x8, matrix products, window_update(): jnp.dot(mixed, w_out, preferred_element_type=jnp.float32) * ocean[:, None]  15.4 us
    dot_general x8, matrix products, window_update(): projected = jnp.dot(normed, w_qkv, preferred_element_type=jnp.float32)  11.3 us
  transfers between devices with their start and end apart: 16, of which 13 were waited for; matrix products, arithmetic and copies ran while one was open for 0% of the time, Pallas kernels for 0%

commit v1 on v0

v1 whole, which is shorter than its diff:
```python
import functools

import jax
import jax.numpy as jnp
from jax import lax
from jax.experimental import pallas as pl
from jax.experimental.pallas import tpu as pltpu
from jax.sharding import PartitionSpec as P

C = 256
HEADS = 8
HEAD = C // HEADS
W = 16
SHIFT = 8
LEV = 2
HALF = W * W * LEV // 2
BLK = HALF // 2
QB = 32
ONES = 16
SMALL = 160
LAND = 1024.0
SAFE_SQ = 60.0**2

VMEM = pl.BlockSpec(memory_space=pltpu.VMEM)
SMEM = pl.BlockSpec(memory_space=pltpu.SMEM)
ANY = pl.BlockSpec(memory_space=pl.ANY)
PARAMS = pltpu.CompilerParams(vmem_limit_bytes=36 * 1024 * 1024)


def dot_nt(a, b):
    return lax.dot_general(a, b, (((1,), (1,)), ((), ())), preferred_element_type=jnp.float32)


def dot_nn(a, b):
    return jnp.dot(a, b, preferred_element_type=jnp.float32)


def iota(shape, axis):
    return lax.broadcasted_iota(jnp.int32, shape, axis)


def one(condition):
    return jnp.where(condition, 1.0, 0.0).astype(jnp.bfloat16)


def ocean_ranks(halves, rows_n):
    channel, row = iota((rows_n, C), 1), iota((rows_n, C), 0)
    marks = None
    for i, half in enumerate(halves):
        part = dot_nt(one((channel == 0) & (row == i)), half)
        marks = part if marks is None else marks + part
    ocean = jnp.where(marks < LAND / 2, 1.0, 0.0)
    return dot_nn(ocean.astype(jnp.bfloat16), one(iota((C, C), 0) <= iota((C, C), 1))) * ocean


def packed_norm(tokens, ranks, count, size, gain):
    wanted = jnp.minimum(iota((size, 1), 0) + 1, count).astype(jnp.float32)
    packed = dot_nn(one(ranks == wanted), tokens)
    average = jnp.mean(packed, axis=1, keepdims=True)
    centred = packed - average
    spread_sq = jnp.mean(centred * centred, axis=1, keepdims=True)
    return (centred * lax.rsqrt(spread_sq + 1e-05) * gain).astype(jnp.bfloat16)


def valid_values(values, count, size):
    valid = iota((1, size), 1) < count
    return jnp.where(valid, values, 0.0).astype(jnp.bfloat16), one(jnp.broadcast_to(valid, (ONES, size)))


def head_norms(keys, sums):
    return jnp.max(dot_nn((keys * keys).astype(jnp.bfloat16), sums), axis=0, keepdims=True)


def fill(keys, values, i, key, size):
    keys[i, size:, :] = jnp.broadcast_to(key[0:1].astype(jnp.float32), (HALF - size, C)).astype(jnp.bfloat16)
    values[i, :, size:] = jnp.zeros((C + ONES, HALF - size), jnp.bfloat16)


def prep_kernel(flags, state, mask, part_a, part_b, held, sems):
    blocks = part_a.shape[0]
    cols = blocks * SHIFT
    half = SHIFT // 2
    chunks = [(s, level, g) for s in range(2) for level in range(LEV) for g in range(2)]
    copies = []
    for i, (s, level, g) in enumerate(chunks):
        start = jnp.where(flags[2] == s, SHIFT, 0) + half * g
        copies.append(pltpu.make_async_copy(state.at[level, pl.ds(start, half)], held.at[i], sems.at[i]))
        copies[-1].start()
    eye = one(iota((cols, cols), 0) == iota((cols, cols), 1))
    by_column = [dot_nt(eye, mask[level].astype(jnp.float32).astype(jnp.bfloat16)) for level in range(LEV)]
    for i, (s, level, g) in enumerate(chunks):
        part = (part_a, part_b)[s]
        upper = flags[2] == s
        copies[i].wait()
        for p in range(half // 2):
            pair = []
            for row in (2 * p, 2 * p + 1):
                at = half * g + row
                ocean = jnp.where(upper, by_column[level][:, SHIFT + at : SHIFT + at + 1], by_column[level][:, at : at + 1])
                pair.append(jnp.where(ocean > 0.5, held[i, row].astype(jnp.float32), LAND).reshape(blocks, SHIFT, C))
            at = (BLK // 2) * level + SHIFT * (half * g + 2 * p)
            part[:, at : at + 2 * SHIFT, :] = jnp.concatenate(pair, axis=1).astype(jnp.bfloat16)


def prep(flags, state, mask):
    blocks = state.shape[2] // SHIFT
    shape = jax.ShapeDtypeStruct((blocks, BLK, C), jnp.bfloat16)
    return pl.pallas_call(
        prep_kernel,
        out_shape=(shape, shape),
        in_specs=[SMEM, ANY, VMEM],
        out_specs=(VMEM, VMEM),
        scratch_shapes=[
            pltpu.VMEM((2 * LEV * 2, SHIFT // 2, state.shape[2], C), jnp.bfloat16),
            pltpu.SemaphoreType.DMA((2 * LEV * 2,)),
        ],
        compiler_params=pltpu.CompilerParams(vmem_limit_bytes=58 * 1024 * 1024),
        name="windows_prep",
    )(flags, state, mask)


def edge_parts(flags, state, mask, start):
    cut = jnp.where(mask[:, :, start : start + SHIFT, None] > 0, state[:, :, start : start + SHIFT], jnp.bfloat16(LAND))
    lower, upper = [cut[:, SHIFT * r : SHIFT * r + SHIFT].reshape(BLK, C) for r in range(2)]
    odd = flags[2] == 1
    return jnp.stack([jnp.where(odd, lower, upper), jnp.where(odd, upper, lower)])


def finish_kernel(flags, state, inner, outer, out):
    level, r = pl.program_id(0), pl.program_id(1)
    s = jnp.where(r == 1, flags[2], 1 - flags[2])
    blocks = state.shape[2] // SHIFT
    for p in range(SHIFT // 2):
        at = pl.multiple_of(level * (BLK // 2) + 2 * SHIFT * p, 2 * SHIFT)
        deltas = []
        for b in range(blocks):
            if b == 0 or b == blocks - 1:
                delta = outer[b // (blocks - 1), s, 0, pl.ds(at, 2 * SHIFT), :]
            else:
                delta = inner[(b - 1) // 2, s, (b - 1) % 2, pl.ds(at, 2 * SHIFT), :]
            deltas.append(delta.astype(jnp.float32))
        for i in range(2):
            added = jnp.concatenate([d[SHIFT * i : SHIFT * i + SHIFT] for d in deltas], axis=0)
            out[0, 2 * p + i] = (state[0, 2 * p + i].astype(jnp.float32) + added).astype(jnp.bfloat16)


def finish(flags, state, inner, outer):
    levels, rows, cols, _ = state.shape
    block = pl.BlockSpec((1, SHIFT, cols, C), lambda l, r, flags: (l, r, 0, 0))
    whole = lambda x: pl.BlockSpec(x.shape, lambda l, r, flags: (0,) * x.ndim)
    return pl.pallas_call(
        finish_kernel,
        out_shape=jax.ShapeDtypeStruct(state.shape, state.dtype),
        grid_spec=pltpu.PrefetchScalarGridSpec(
            num_scalar_prefetch=1,
            grid=(levels, 2),
            in_specs=[block, pl.BlockSpec(memory_space=pltpu.VMEM), pl.BlockSpec(memory_space=pltpu.VMEM)],
            out_specs=block,
        ),
        compiler_params=PARAMS,
        name="windows_finish",
    )(flags, state, inner, outer)


def near_kernel(edges, n, part_a, part_b, west, east, gain, w_qkv, k_out, vt_out, qt_out, spread_out, counts, peaks, edge, ranks, wqt, wvt, norms):
    parts = (part_a, part_b)
    last = part_a.shape[0] - 1
    if edges:
        for s in range(2):
            edge[s, 0], edge[s, 1] = parts[s][0], west[s]
            edge[s, 2], edge[s, 3] = parts[s][last], east[s]

    def tokens_at(w, s):
        if edges:
            return edge[s, pl.ds(2 * w, 2)].reshape(HALF, C)
        return parts[s][pl.ds(2 * w + 1, 2)].reshape(HALF, C)

    rank = ocean_ranks([tokens_at(i // 2, i % 2) for i in range(2 * n)], 16)
    ranks[...] = rank
    for i in range(2 * n):
        counts[i] = jnp.max(rank[i : i + 1, :]).astype(jnp.int32)
        counts[2 * n + i] = jnp.max(rank[i : i + 1, :BLK]).astype(jnp.int32) if edges else counts[i]

    eye = one(iota((C, C), 0) == iota((C, C), 1))
    wqt[...] = dot_nt(eye, w_qkv[:, :C]).astype(jnp.bfloat16)
    wvt[...] = dot_nt(eye, w_qkv[:, 2 * C :]).astype(jnp.bfloat16)
    norms[...] = jnp.zeros_like(norms)
    by_column = dot_nt(eye, rank.astype(jnp.bfloat16))
    for i in range(2 * n):
        col_rank = jnp.broadcast_to(by_column[:, i : i + 1], (HALF, BLK))
        for at in (0, BLK):
            number = (iota((HALF, BLK), 1) + (at + 1)).astype(jnp.float32)
            spread_out[i, :, at : at + BLK] = one(col_rank == number)

    def window(size, w):
        sums = one(iota((C, BLK), 0) // HEAD == iota((C, BLK), 1))
        sums_t = one(iota((ONES, C), 1) // HEAD == iota((ONES, C), 0))
        count = [counts[2 * w + s] for s in range(2)]
        normed = [
            packed_norm(tokens_at(w, s), ranks[pl.ds(2 * w + s, 1), :], count[s], size, gain[...]) for s in range(2)
        ]
        keys = [dot_nn(x, w_qkv[:, C : 2 * C]).astype(jnp.bfloat16) for x in normed]
        queries = [(dot_nt(wqt[...], x) * (1.0 / HEAD**0.5)).astype(jnp.bfloat16) for x in normed]
        values = [valid_values(dot_nt(wvt[...], x), c, size) for x, c in zip(normed, count)]
        for s in range(2):
            k_out[2 * w + s, :size, :] = keys[s]
            qt_out[2 * w + s, :, :size] = queries[s]
            vt_out[2 * w + s, :C, :size] = values[s][0]
            vt_out[2 * w + s, C:, :size] = values[s][1]
            if size < HALF:
                qt_out[2 * w + s, :, size:] = jnp.zeros((C, HALF - size), jnp.bfloat16)
                fill(k_out, vt_out, 2 * w + s, keys[s], size)
            norms[0:1, :] = jnp.maximum(norms[0:1, :], head_norms(keys[s], sums))
            by_head = dot_nn(sums_t, queries[s] * queries[s])
            norms[8:, :] = jnp.maximum(norms[8:, :], jnp.max(by_head, axis=1, keepdims=True))

    def either(w, carry):
        largest = jnp.maximum(counts[2 * w], counts[2 * w + 1])
        for size, fits in ((SMALL, largest <= SMALL), (HALF, largest > SMALL)):
            pl.when(fits)(functools.partial(window, size, w))
        return carry

    lax.fori_loop(0, n, either, 0)
    peaks[0] = jnp.max(norms[0:1, :])
    peaks[1] = jnp.max(norms[8:, :])


def near_half(edges, part_a, part_b, west, east, gain, w_qkv):
    n = 2 if edges else part_a.shape[0] // 2 - 1
    bf = lambda *shape: jax.ShapeDtypeStruct(shape, jnp.bfloat16)
    return pl.pallas_call(
        functools.partial(near_kernel, edges, n),
        out_shape=(
            bf(2 * n, HALF, C),
            bf(2 * n, C + ONES, HALF),
            bf(2 * n, C, HALF),
            bf(2 * n, HALF, HALF),
            jax.ShapeDtypeStruct((4 * n,), jnp.int32),
            jax.ShapeDtypeStruct((2,), jnp.float32),
        ),
        in_specs=[VMEM] * 6,
        out_specs=(VMEM,) * 4 + (SMEM,) * 2,
        scratch_shapes=[
            pltpu.VMEM((2, 4, BLK, C), jnp.bfloat16),
            pltpu.VMEM((16, C), jnp.float32),
            pltpu.VMEM((C, C), jnp.bfloat16),
            pltpu.VMEM((C, C), jnp.bfloat16),
            pltpu.VMEM((8 + ONES, BLK), jnp.float32),
        ],
        compiler_params=PARAMS,
        cost_estimate=pl.CostEstimate(flops=n * 10**9, bytes_accessed=n * 10**6, transcendentals=0),
        name="windows_near_edge" if edges else "windows_near",
    )(part_a, part_b, west, east, gain, w_qkv)


def tops(scores, bounded):
    if bounded:
        return scores
    top = jnp.maximum(jnp.max(scores[0], axis=0, keepdims=True), jnp.max(scores[1], axis=0, keepdims=True))
    return [score - top for score in scores]


def mix(scores, values, slots, queries_n):
    parts = [dot_nn(value, jnp.exp(score).astype(jnp.bfloat16)) for score, value in zip(scores, values)]
    summed = parts[0] + parts[1]
    n = summed.shape[0] - ONES
    total = summed[n : n + 1, :] + jnp.where(slots < queries_n, 0.0, 1.0)
    return summed[:n, :] * (1.0 / total)


def far_kernel(
    edges, n, flags, counts, peaks, far_a, far_b, corner_a, corner_b, gain, w_qkv, w_out, k_near, vt_near, qt, spread, out,
    edge, ranks, k_far, vt_far, wvt, woutt, norms, rem, mixes, count_far,
):
    far_refs, corners = (far_a, far_b), (corner_a, corner_b)
    last = far_a.shape[0] - 1
    top = flags[1]
    if edges:
        for s in range(2):
            for e in range(2):
                i = jnp.where(top == 1, 1 - e, e) if s == 1 else e
                edge[s, 2 * e] = far_refs[s][last * i]
                edge[s, 2 * e + 1] = corners[s][i]

    def tokens_at(w, s):
        if edges:
            return edge[s, pl.ds(2 * w, 2)].reshape(HALF, C)
        i = jnp.where(top == 1, n - 1 - w, w) if s == 1 else w
        return far_refs[s][pl.ds(2 * i + 1, 2)].reshape(HALF, C)

    rank = ocean_ranks([tokens_at(i // 2, i % 2) for i in range(2 * n)], 16)
    ranks[...] = rank
    for i in range(2 * n):
        found = jnp.max(rank[i : i + 1, :]).astype(jnp.int32)
        count_far[i] = jnp.where(flags[0] == 1, 0, found) if i % 2 else found
    eye = one(iota((C, C), 0) == iota((C, C), 1))
    wvt[...] = dot_nt(eye, w_qkv[:, 2 * C :]).astype(jnp.bfloat16)
    woutt[...] = dot_nt(eye, w_out[...]).astype(jnp.bfloat16)
    norms[...] = jnp.zeros_like(norms)

    def both(j):
        windows = (2 * j, jnp.minimum(2 * j + 1, n - 1))
        return [(w, s) for w in windows for s in range(2)]

    def prepare(size, j):
        sums = one(iota((C, BLK), 0) // HEAD == iota((C, BLK), 1))
        items = both(j)
        count = [count_far[2 * w + s] for w, s in items]
        normed = [
            packed_norm(tokens_at(w, s), ranks[pl.ds(2 * w + s, 1), :], c, size, gain[...]) for (w, s), c in zip(items, count)
        ]
        keys = [dot_nn(x, w_qkv[:, C : 2 * C]) for x in normed]
        values = [valid_values(dot_nt(wvt[...], x), c, size) for x, c in zip(normed, count)]
        for (w, s), c, key, value in zip(items, count, keys, values):
            spare = jnp.broadcast_to(k_near[2 * w + s, 0:1, :].astype(jnp.float32), (size, C))
            key = jnp.where(c > 0, key, spare).astype(jnp.bfloat16)
            k_far[2 * w + s, :size, :] = key
            vt_far[2 * w + s, :C, :size] = value[0]
            vt_far[2 * w + s, C:, :size] = value[1]
            if size < HALF:
                fill(k_far, vt_far, 2 * w + s, key, size)
            norms[0:1, :] = jnp.maximum(norms[0:1, :], head_norms(key, sums))

    def ready(j, carry):
        largest = functools.reduce(jnp.maximum, [count_far[2 * w + s] for w, s in both(j)])
        for size, fits in ((SMALL, largest <= SMALL), (HALF, largest > SMALL)):
            pl.when(fits)(functools.partial(prepare, size, j))
        return carry

    lax.fori_loop(0, (n + 1) // 2, ready, 0)
    peak = jnp.maximum(jnp.max(norms[0:1, :]), peaks[0]) * peaks[1]
    safe = peak <= SAFE_SQ

    lane = iota((1, C), 1)

    def attend(w, halves, size, bounded):
        asked = {s: counts[2 * n + 2 * w + s] for s in halves}
        at = {s: 2 * w + s for s in halves}
        keys = {s: [k_near[at[s], :size, :], k_far[2 * w + s, :size, :]] for s in halves}

        def values(s, rows):
            return [
                jnp.concatenate([ref[i, rows, :size], ref[i, C : C + ONES, :size]], axis=0)
                for ref, i in ((vt_near, at[s]), (vt_far, 2 * w + s))
            ]

        def tile_scores(t, s):
            g = t // 2
            none = jnp.zeros((HEAD, BLK), jnp.bfloat16)
            rows = []
            for h in range(4 * g, 4 * g + 4):
                mine = qt[at[s], HEAD * h : HEAD * h + HEAD, :BLK] if h // 2 == t else none
                rows.append(jnp.concatenate([mine, none] if h % 2 == 0 else [none, mine], axis=1))
            stacked = jnp.concatenate(rows, axis=0)
            return [dot_nn(key[:, BLK * g : BLK * g + BLK], stacked) for key in keys[s]]

        tiles = [(t, s) for t in range(4) for s in halves]
        ahead = tile_scores(*tiles[0])
        for i, (t, s) in enumerate(tiles):
            now = ahead
            if i + 1 < len(tiles):
                ahead = tile_scores(*tiles[i + 1])
            mixed = mix(tops(now, bounded), values(s, slice(64 * t, 64 * t + 64)), lane % BLK, asked[s])
            mixes[2 * w + s, 64 * t : 64 * t + HEAD, :BLK] = mixed[:HEAD, :BLK].astype(jnp.bfloat16)
            mixes[2 * w + s, 64 * t + HEAD : 64 * t + 64, :BLK] = mixed[HEAD:, BLK:].astype(jnp.bfloat16)

        most = functools.reduce(jnp.maximum, asked.values())
        for s in halves:
            rem[s] = jnp.zeros_like(rem[s])

        def more(b, carry):
            start = b * QB
            sub, lan = iota((C, C), 0), iota((C, C), 1)
            block = sub // HEAD == lan // QB
            repeat = one(sub[:BLK] + BLK == start + lan[:BLK] % QB)
            place = one(sub[:, :BLK] % QB + start == lan[:, :BLK] + BLK)
            stacked = [jnp.where(block, dot_nn(qt[at[s], :, BLK:], repeat), 0.0).astype(jnp.bfloat16) for s in halves]
            scores = [[dot_nn(key, x) for key in keys[s]] for s, x in zip(halves, stacked)]
            mixed = [
                mix(tops(score, bounded), values(s, slice(0, C)), start + lane % QB, asked[s]) for s, score in zip(halves, scores)
            ]
            mixed = [jnp.where(block, x, 0.0).astype(jnp.bfloat16) for x in mixed]
            placed = [dot_nn(x, place) for x in mixed]
            for s, x in zip(halves, placed):
                rem[s] = (rem[s].astype(jnp.float32) + x).astype(jnp.bfloat16)
            return carry

        lax.fori_loop(BLK // QB, (most + QB - 1) // QB, more, 0)
        for s in halves:
            mixes[2 * w + s, :, BLK:] = rem[s]

    def window(w, carry):
        at = 2 * w
        largest = jnp.maximum(jnp.maximum(counts[at], counts[at + 1]), jnp.maximum(count_far[2 * w], count_far[2 * w + 1]))
        active = jnp.maximum(counts[2 * n + at], counts[2 * n + at + 1]) > 0

        @pl.when(jnp.logical_not(active))
        def _():
            for s in range(2):
                mixes[2 * w + s] = jnp.zeros_like(mixes[2 * w + s])

        pl.when(active & safe & (largest <= SMALL))(functools.partial(attend, w, (0, 1), SMALL, True))
        pl.when(active & safe & (largest > SMALL))(functools.partial(attend, w, (0, 1), HALF, True))
        for s in range(2):
            pl.when(active & jnp.logical_not(safe))(functools.partial(attend, w, (s,), HALF, False))
        return carry

    lax.fori_loop(0, n, window, 0)

    def project(j, carry):
        items = both(j)
        delta_t = [dot_nn(woutt[...], mixes[2 * w + s]).astype(jnp.bfloat16) for w, s in items]
        delta = [dot_nt(spread[2 * w + s], x) for (w, s), x in zip(items, delta_t)]
        for (w, s), x in zip(items, delta):
            if s == 1:
                x = jnp.where(flags[0] == 1, 0.0, x)
            out[w, s] = x.astype(jnp.bfloat16).reshape(2, BLK, C)
        return carry

    lax.fori_loop(0, (n + 1) // 2, project, 0)


def far_half(edges, flags, near, far_a, far_b, corner_a, corner_b, gain, w_qkv, w_out):
    k_near, vt_near, qt, spread, counts, peaks = near
    n = counts.shape[0] // 4
    return pl.pallas_call(
        functools.partial(far_kernel, edges, n),
        out_shape=jax.ShapeDtypeStruct((n, 2, 2, BLK, C), jnp.bfloat16),
        in_specs=[SMEM] * 3 + [VMEM] * 11,
        out_specs=VMEM,
        scratch_shapes=[
            pltpu.VMEM((2, 4, BLK, C), jnp.bfloat16),
            pltpu.VMEM((16, C), jnp.float32),
            pltpu.VMEM((2 * n, HALF, C), jnp.bfloat16),
            pltpu.VMEM((2 * n, C + ONES, HALF), jnp.bfloat16),
            pltpu.VMEM((C, C), jnp.bfloat16),
            pltpu.VMEM((C, C), jnp.bfloat16),
            pltpu.VMEM((8, BLK), jnp.float32),
            pltpu.VMEM((2, C, BLK), jnp.bfloat16),
            pltpu.VMEM((2 * n, C, HALF), jnp.bfloat16),
            pltpu.SMEM((2 * n,), jnp.int32),
        ],
        compiler_params=PARAMS,
        cost_estimate=pl.CostEstimate(flops=n * 10**9, bytes_accessed=n * 10**6, transcendentals=0),
        name="windows_edge" if edges else "windows_inner",
    )(flags, counts, peaks, far_a, far_b, corner_a, corner_b, gain, w_qkv, w_out, k_near, vt_near, qt, spread)


def permute(x, pairs):
    return lax.ppermute(x, ("lon", "lat"), pairs)


def shards(state, ocean_mask, norm_gain, w_qkv, w_out):
    lon_n, lat_n = lax.axis_size("lon"), lax.axis_size("lat")
    lat = lax.axis_index("lat")
    at = lambda i, j: i * lat_n + j
    every = [(i, j) for i in range(lon_n) for j in range(lat_n)]
    go_a = [(at(i, j), at(i, j - 1 if j % 2 else j + 1)) for i, j in every]
    go_b = [(at(i, j), at(i, j + 1 if j % 2 else j - 1)) for i, j in every if 0 < j < lat_n - 1]
    go_b += [(at(i, lat_n - 1), at(lon_n - 1 - i, lat_n - 1)) for i in range(lon_n)]
    go_east = [(at(i, j), at((i + 1) % lon_n, j)) for i, j in every]
    go_west = [(at(i, j), at((i - 1) % lon_n, j)) for i, j in every]

    flags = jnp.stack([lat == 0, lat == lat_n - 1, lat % 2 == 1]).astype(jnp.int32)
    west = permute(edge_parts(flags, state, ocean_mask, state.shape[2] - SHIFT), go_east)
    east = permute(edge_parts(flags, state, ocean_mask, 0), go_west)
    part_a, part_b = prep(flags, state, ocean_mask)
    far_a = permute(part_a, go_a)
    far_b = permute(part_b, go_b)

    gain = norm_gain[None, :]
    near = near_half(False, part_a, part_b, part_a, part_b, gain, w_qkv)
    near_edge = near_half(True, part_a, part_b, west, east, gain, w_qkv)
    west, east, near, near_edge = lax.optimization_barrier((west, east, near, near_edge))
    corner_a = permute(jnp.stack([west[0], east[0]]), go_a)
    corner_b = permute(jnp.stack([west[1], east[1]]), go_b)
    inner = far_half(False, flags, near, far_a, far_b, far_a, far_b, gain, w_qkv, w_out)
    inner, near_edge = lax.optimization_barrier((inner, near_edge))
    outer = far_half(True, flags, near_edge, far_a, far_b, corner_a, corner_b, gain, w_qkv, w_out)
    return finish(flags, state, inner, outer)


def solution(mesh):
    in_specs = (P(None, "lat", "lon", None), P(None, "lat", "lon"), P(), P(), P())
    out_specs = P(None, "lat", "lon", None)
    return jax.shard_map(shards, mesh=mesh, in_specs=in_specs, out_specs=out_specs, check_vma=False)
```

time: 316 us -> 81.5 us (0.26); the launches traced: 313 us -> 82.2 us
  matrix products: 113 us -> 0 us
  waiting for transfers between devices: 115 us -> 5.89 us
  Pallas kernels: 0 us -> 55.1 us
  other arithmetic: 27.1 us -> 2.14 us
  local copies, waits for them, and re-layouts: 26.3 us -> 3.1 us
  starting transfers between devices: 29.5 us -> 15 us
    dot_general x144 -> x0, matrix products: 113 us -> none  [the longest x64 63 us: one_head(): jnp.dot(weights.astype(jnp.bfloat16), value_h, preferred_element_type=jnp...]
    ppermute x16 -> x6, waiting for transfers between devices: 115 us -> 5.89 us  [permute(): return lax.ppermute(x, ('lon', 'lat'), pairs)]
    pallas_call x0 -> x6, Pallas kernels: none -> 55.1 us  [the longest x2 36.9 us: far_half(): pl.pallas_call(functools.partial(far_kernel, edges, n), out_shape=jax.Sha...]
    reduce_sum x80 -> x0, other arithmetic: 22 us -> none  [the longest x64 19 us: one_head(): total = jnp.sum(weights, axis=1) + (1.0 - ocean)]
    ppermute x16 -> x6, starting transfers between devices: 29.5 us -> 15 us  [permute(): return lax.ppermute(x, ('lon', 'lat'), pairs)]
    reshape x6 -> x0, local copies, waits for them, and re-layouts: 10.8 us -> none  [the longest x1 4.57 us: to_windows(): shaped = grid.reshape((levels_n, rows_n // W, W, cols_n // W, W) + rest)]
    while x33 -> x0, local copies, waits for them, and re-layouts: 7.51 us -> none
    slice x28 -> x3, local copies, waits for them, and re-layouts: 5.47 us -> 0.61 us  [the longest x1 0.58 us: edge_parts(): odd = flags[2] == 1]
  transfers between devices with their start and end apart: 16 -> 6, of which waited for: 13 -> 1; matrix products, arithmetic and copies ran while one was open for 0% -> 0% of each run, Pallas kernels for 0% -> 55%
where the time goes in v1:
time: 81.5 us; the launch traced here: 82.2 us
  Pallas kernels  55.1 us (68%)
  starting transfers between devices  15 us (18%)
  waiting for transfers between devices  5.89 us (7%)
  local copies, waits for them, and re-layouts  3.1 us (4%)
  other arithmetic  2.14 us (3%)
  between operations  0.89 us (1%)
    pallas_call x2, Pallas kernels, far_half(): pl.pallas_call(functools.partial(far_kernel, edges, n), out_shape=jax.Sha...  36.9 us
    ppermute x6, starting transfers between devices, permute(): return lax.ppermute(x, ('lon', 'lat'), pairs)  15 us
    pallas_call x2, Pallas kernels, near_half(): pl.pallas_call(functools.partial(near_kernel, edges, n), out_shape=(bf(2...  11.4 us
    ppermute x6, waiting for transfers between devices, permute(): return lax.ppermute(x, ('lon', 'lat'), pairs)  5.89 us
    pallas_call x1, Pallas kernels, prep(): pl.pallas_call(prep_kernel, out_shape=(shape, shape), in_specs=[SMEM, ANY...  4.23 us
    pallas_call x1, Pallas kernels, finish(): pl.pallas_call(finish_kernel, out_shape=jax.ShapeDtypeStruct(state.shape,...  2.58 us
    unnamed x16, local copies, waits for them, and re-layouts  2.5 us
  transfers between devices with their start and end apart: 6, of which 1 were waited for; matrix products, arithmetic and copies ran while one was open for 0% of the time, Pallas kernels for 55%

profile of v1, /device:TPU:224, one launch (start us, length us, event | category | flops | bytes accessed | tf_op | source)
XLA Modules:
  0.0 82.2 jit_solution(6699965337149483663)
XLA Ops:
  0.0 0.0 copy-start.7
  0.0 0.0 copy-start.5
  0.0 0.1 add_convert_fusion.flags
  0.1 0.0 copy-start.1
  0.1 0.6 slice.40
  0.7 0.9 %slice_compare_fusion = (pred[2,16,8]{2,1,0:T(8,128)(4,1)S(1)}, pred[2,16,8]{2,1,0:T(8,128)(4,1)S(1)}) fusion(s32[2,16,128]{2,1,0:T(8,128)} %mask.1), kind=kLoop, calls=%fused_computation.10 | loop fusion | flops 512 | bytes 2560 | tf_op jit(solution)/shard_map/gt | solution.py:123
  2.2 1.1 %slice_select_fusion = (bf16[2,16,8,256]{3,2,1,0:T(8,128)(2,1)S(1)}, bf16[2,16,8,256]{3,2,1,0:T(8,128)(2,1)S(1)}) fusion(bf16[2,16,128,256]{3,2,1,0:T(8,128)(2,1)} %state.3, pred[2,16,8]{2,1,0:T(8,128)(4,1)S(1)} %get-tuple-element.85, pred[2,16,8]{2,1,0:T(8,128)(4,1)S(1)} %get-tuple-element.86), kind=kLoop, calls=%fused_computation.4 | loop fusion | flops 131072 | bytes 524800 | tf_op jit(solution)/shard_map/jit(_where)/select_n | solution.py:123
  3.4 4.7 %collective-permute-start.1 = (bf16[2,128,256]{2,1,0:T(8,128)(2,1)S(1)}, bf16[2,128,256]{2,1,0:T(8,128)(2,1)S(1)}, u32[]{:S(2)}, u32[]{:S(2)}) collective-permute-start(bf16[2,128,256]{2,1,0:T(8,128)(2,1)S(1)} %pad_maximum_fusion.1), channel_id=1, source_target_pairs={{0,248},{1,249},{2,250},{3,251},{4,252},{5,253},{6,254},{7,255},{8... | collective-permute-start | bytes 393224 | tf_op jit(solution)/shard_map/ppermute | solution.py:450
  8.1 0.1 collective-permute-start
  8.2 0.0 copy-done.1
  8.2 4.2 %windows_prep.1 = (bf16[16,128,256]{2,1,0:T(8,128)(2,1)}, bf16[16,128,256]{2,1,0:T(8,128)(2,1)}) custom-call(s32[3]{0:T(128)} %copy-done.1, bf16[2,16,128,256]{3,2,1,0:T(8,128)(2,1)} %state.3, s32[2,16,128]{2,1,0:T(8,128)} %mask.1), custom_call_target="tpu_custom_call" | custom-call | tf_op jit(solution)/shard_map/windows_prep/pallas_call | solution.py:108
  12.4 1.1 %collective-permute-start.2 = (bf16[16,128,256]{2,1,0:T(8,128)(2,1)}, bf16[16,128,256]{2,1,0:T(8,128)(2,1)S(1)}, u32[]{:S(2)}, u32[]{:S(2)}) collective-permute-start(bf16[16,128,256]{2,1,0:T(8,128)(2,1)} %get-tuple-element.40.part_a.west), channel_id=1, source_target_pairs={{0,1},{1,0},{2,3},{3,2},{4,5},{5,4},{6,7},{7,6},{8,9},{9,8},{10,11... | collective-permute-start | bytes 3145736 | tf_op jit(solution)/shard_map/ppermute | solution.py:450
  13.5 6.7 %collective-permute-start.3 = (bf16[16,128,256]{2,1,0:T(8,128)(2,1)}, bf16[16,128,256]{2,1,0:T(8,128)(2,1)S(1)}, u32[]{:S(2)}, u32[]{:S(2)}) collective-permute-start(bf16[16,128,256]{2,1,0:T(8,128)(2,1)} %get-tuple-element.41.part_b.east), channel_id=1, source_target_pairs={{1,2},{2,1},{3,4},{4,3},{5,6},{6,5},{9,10},{10,9},{11,12},{12,11},... | collective-permute-start | bytes 3145736 | tf_op jit(solution)/shard_map/ppermute | solution.py:450
  20.2 0.0 copy-done.7
  20.2 0.0 copy-done.5
  20.2 0.0 copy-start.3
  20.2 1.2 %copy-done.3 = bf16[16,128,256]{2,1,0:T(8,128)(2,1)S(1)} copy-done((bf16[16,128,256]{2,1,0:T(8,128)(2,1)S(1)}, bf16[16,128,256]{2,1,0:T(8,128)(2,1)}, u32[]{:S(2)}) %copy-start.3) | copy-done | bytes 1048600
  21.5 0.0 copy-start.4
  21.5 1.2 %copy-done.4 = bf16[16,128,256]{2,1,0:T(8,128)(2,1)S(1)} copy-done((bf16[16,128,256]{2,1,0:T(8,128)(2,1)S(1)}, bf16[16,128,256]{2,1,0:T(8,128)(2,1)}, u32[]{:S(2)}) %copy-start.4) | copy-done | bytes 1048600
  22.7 8.1 %windows_near.1 = (bf16[14,256,256]{2,1,0:T(8,128)(2,1)S(1)}, bf16[14,272,256]{2,1,0:T(8,128)(2,1)S(1)}, bf16[14,256,256]{2,1,0:T(8,128)(2,1)S(1)}, bf16[14,256,...) custom-call(bf16[16,128,256]{2,1,0:T(8,128)(2,1)S(1)} %copy-done.4, bf16[16,128,256]{2,1,0:T(8,128)(2,1)S(1)} %copy-done.3, ...), custom_call_target="tpu_custom_call" | custom-call | flops 7000000000 | bytes 7000000 | tf_op jit(solution)/shard_map/windows_near/pallas_call | solution.py:231
  30.8 0.0 copy-start.2
  30.9 0.0 copy-start.6
  30.9 0.0 collective-permute-done.1.east
  30.9 0.0 collective-permute-done.west
  30.9 3.3 %windows_near_edge.1 = (bf16[4,256,256]{2,1,0:T(8,128)(2,1)S(1)}, bf16[4,272,256]{2,1,0:T(8,128)(2,1)S(1)}, bf16[4,256,256]{2,1,0:T(8,128)(2,1)S(1)}, bf16[4,256...) custom-call(bf16[16,128,256]{2,1,0:T(8,128)(2,1)S(1)} %copy-done.4, bf16[16,128,256]{2,1,0:T(8,128)(2,1)S(1)} %copy-done.3, ...), custom_call_target="tpu_custom_call" | custom-call | flops 2000000000 | bytes 2000000 | tf_op jit(solution)/shard_map/windows_near_edge/pallas_call | solution.py:231
  34.3 2.2 %collective-permute-start.5 = (bf16[2,128,256]{2,1,0:T(8,128)(2,1)S(1)}, bf16[2,128,256]{2,1,0:T(8,128)(2,1)S(1)}, u32[]{:S(2)}, u32[]{:S(2)}) collective-permute-start(bf16[2,128,256]{2,1,0:T(8,128)(2,1)S(1)} %pad_maximum_fusion.3), channel_id=1, source_target_pairs={{1,2},{2,1},{3,4},{4,3},{5,6},{6,5},{9,10},{10,9},{11,12},{12,11},... | collective-permute-start | bytes 393224 | tf_op jit(solution)/shard_map/ppermute | solution.py:450
  36.5 0.3 collective-permute-start.4
  36.8 0.0 collective-permute-done.2.far_a.corner_a
  36.8 5.9 %collective-permute-done.3.far_b.corner_b = bf16[16,128,256]{2,1,0:T(8,128)(2,1)S(1)} collective-permute-done((bf16[16,128,256]{2,1,0:T(8,128)(2,1)}, bf16[16,128,256]{2,1,0:T(8,128)(2,1)S(1)}, u32[]{:S(2)}, u32[]{:S(2)}) %collective-permute-start.3) | collective-permute-done | bytes 1048608 | tf_op jit(solution)/shard_map/ppermute | solution.py:450
  42.7 0.0 copy-done.2
  42.7 0.0 copy-done.6
  42.7 29.7 %windows_inner.1.inner = bf16[7,2,2,128,256]{4,3,2,1,0:T(8,128)(2,1)S(1)} custom-call(s32[3]{0:T(128)S(1)} %copy-done.2, s32[28]{0:T(128)S(1)} %get-tuple-element.54.counts, f32[2]{0:T(128)S(1)} %get-tuple-element.55.peaks, bf16[16,128,256]{2,1,0:T(8,128)(2,1)S(1)} %collective-permute-done.2.far_a.corner_a, ...), custom_call_target="tpu_custom_call" | custom-call | flops 7000000000 | bytes 7000000 | tf_op jit(solution)/shard_map/windows_inner/pallas_call | solution.py:426
  72.4 0.0 copy-start
  72.4 0.0 collective-permute-done.5.corner_b
  72.4 0.0 collective-permute-done.4.corner_a
  72.4 7.2 %windows_edge.1.outer = bf16[2,2,2,128,256]{4,3,2,1,0:T(8,128)(2,1)S(1)} custom-call(s32[3]{0:T(128)S(1)} %copy-done.2, s32[8]{0:T(128)S(1)} %get-tuple-element.67.counts, f32[2]{0:T(128)S(1)} %get-tuple-element.68.peaks, bf16[16,128,256]{2,1,0:T(8,128)(2,1)S(1)} %collective-permute-done.2.far_a.corner_a, ...), custom_call_target="tpu_custom_call" | custom-call | flops 2000000000 | bytes 2000000 | tf_op jit(solution)/shard_map/windows_edge/pallas_call | solution.py:426
  79.6 0.0 copy-done
  79.6 2.6 %windows_finish.1 = bf16[2,16,128,256]{3,2,1,0:T(8,128)(2,1)} custom-call(s32[3]{0:T(128)S(1)} %copy-done.2, bf16[2,16,128,256]{3,2,1,0:T(8,128)(2,1)S(1)} %copy-done, bf16[7,2,2,128,256]{4,3,2,1,0:T(8,128)(2,1)S(1)} %windows_inner.1.inner, bf16[2,2,2,128,256]{4,3,2,1,0:T(8,128)(2,1)S(1)} %windows_edge.1.outer), custom_call_target="tpu_custom_call" | custom-call | tf_op jit(solution)/shard_map/windows_finish/pallas_call | solution.py:151
  (7 shorter events, 0.1 us)
Async XLA Ops:
  0.0 20.2 %copy-start.7 = (f32[256]{0:T(256)S(1)}, f32[256]{0:T(256)}, u32[]{:S(2)}) copy-start(f32[256]{0:T(256)} %param.7) | copy-start | bytes 3076
  0.0 20.2 %copy-start.5 = (bf16[256,768]{1,0:T(8,128)(2,1)S(1)}, bf16[256,768]{1,0:T(8,128)(2,1)}, u32[]{:S(2)}) copy-start(bf16[256,768]{1,0:T(8,128)(2,1)} %w_qkv.7) | copy-start | bytes 1179652
  0.1 8.1 %copy-start.1 = (s32[3]{0:T(128)}, s32[3]{0:T(128)S(1)}, u32[]{:S(2)}) copy-start(s32[3]{0:T(128)S(1)} %add_convert_fusion.flags) | copy-start | bytes 40
  3.4 27.5 %collective-permute-start.1 = (bf16[2,128,256]{2,1,0:T(8,128)(2,1)S(1)}, bf16[2,128,256]{2,1,0:T(8,128)(2,1)S(1)}, u32[]{:S(2)}, u32[]{:S(2)}) collective-permute-start(bf16[2,128,256]{2,1,0:T(8,128)(2,1)S(1)} %pad_maximum_fusion.1), channel_id=1, source_target_pairs={{0,248},{1,249},{2,250},{3,251},{4,252},{5,253},{6,254},{7,255},{8... | collective-permute-start | bytes 393224 | tf_op jit(solution)/shard_map/ppermute | solution.py:450
  8.1 22.8 %collective-permute-start = (bf16[2,128,256]{2,1,0:T(8,128)(2,1)S(1)}, bf16[2,128,256]{2,1,0:T(8,128)(2,1)S(1)}, u32[]{:S(2)}, u32[]{:S(2)}) collective-permute-start(bf16[2,128,256]{2,1,0:T(8,128)(2,1)S(1)} %pad_maximum_fusion), channel_id=1, source_target_pairs={{0,8},{1,9},{2,10},{3,11},{4,12},{5,13},{6,14},{7,15},{8,16},{9,17... | collective-permute-start | bytes 393224 | tf_op jit(solution)/shard_map/ppermute | solution.py:450
  12.4 24.3 %collective-permute-start.2 = (bf16[16,128,256]{2,1,0:T(8,128)(2,1)}, bf16[16,128,256]{2,1,0:T(8,128)(2,1)S(1)}, u32[]{:S(2)}, u32[]{:S(2)}) collective-permute-start(bf16[16,128,256]{2,1,0:T(8,128)(2,1)} %get-tuple-element.40.part_a.west), channel_id=1, source_target_pairs={{0,1},{1,0},{2,3},{3,2},{4,5},{5,4},{6,7},{7,6},{8,9},{9,8},{10,11... | collective-permute-start | bytes 3145736 | tf_op jit(solution)/shard_map/ppermute | solution.py:450
  13.5 29.1 %collective-permute-start.3 = (bf16[16,128,256]{2,1,0:T(8,128)(2,1)}, bf16[16,128,256]{2,1,0:T(8,128)(2,1)S(1)}, u32[]{:S(2)}, u32[]{:S(2)}) collective-permute-start(bf16[16,128,256]{2,1,0:T(8,128)(2,1)} %get-tuple-element.41.part_b.east), channel_id=1, source_target_pairs={{1,2},{2,1},{3,4},{4,3},{5,6},{6,5},{9,10},{10,9},{11,12},{12,11},... | collective-permute-start | bytes 3145736 | tf_op jit(solution)/shard_map/ppermute | solution.py:450
  20.2 1.3 %copy-start.3 = (bf16[16,128,256]{2,1,0:T(8,128)(2,1)S(1)}, bf16[16,128,256]{2,1,0:T(8,128)(2,1)}, u32[]{:S(2)}) copy-start(bf16[16,128,256]{2,1,0:T(8,128)(2,1)} %get-tuple-element.41.part_b.east) | copy-start | bytes 3145732
  21.5 1.2 %copy-start.4 = (bf16[16,128,256]{2,1,0:T(8,128)(2,1)S(1)}, bf16[16,128,256]{2,1,0:T(8,128)(2,1)}, u32[]{:S(2)}) copy-start(bf16[16,128,256]{2,1,0:T(8,128)(2,1)} %get-tuple-element.40.part_a.west) | copy-start | bytes 3145732
  30.8 11.8 %copy-start.2 = (s32[3]{0:T(128)S(1)}, s32[3]{0:T(128)}, u32[]{:S(2)}) copy-start(s32[3]{0:T(128)} %copy-done.1) | copy-start | bytes 40
  30.9 11.8 %copy-start.6 = (bf16[256,256]{1,0:T(8,128)(2,1)S(1)}, bf16[256,256]{1,0:T(8,128)(2,1)}, u32[]{:S(2)}) copy-start(bf16[256,256]{1,0:T(8,128)(2,1)} %w_out.3) | copy-start | bytes 393220
  34.3 38.1 %collective-permute-start.5 = (bf16[2,128,256]{2,1,0:T(8,128)(2,1)S(1)}, bf16[2,128,256]{2,1,0:T(8,128)(2,1)S(1)}, u32[]{:S(2)}, u32[]{:S(2)}) collective-permute-start(bf16[2,128,256]{2,1,0:T(8,128)(2,1)S(1)} %pad_maximum_fusion.3), channel_id=1, source_target_pairs={{1,2},{2,1},{3,4},{4,3},{5,6},{6,5},{9,10},{10,9},{11,12},{12,11},... | collective-permute-start | bytes 393224 | tf_op jit(solution)/shard_map/ppermute | solution.py:450
  36.5 35.9 %collective-permute-start.4 = (bf16[2,128,256]{2,1,0:T(8,128)(2,1)S(1)}, bf16[2,128,256]{2,1,0:T(8,128)(2,1)S(1)}, u32[]{:S(2)}, u32[]{:S(2)}) collective-permute-start(bf16[2,128,256]{2,1,0:T(8,128)(2,1)S(1)} %pad_maximum_fusion.2), channel_id=1, source_target_pairs={{0,1},{1,0},{2,3},{3,2},{4,5},{5,4},{6,7},{7,6},{8,9},{9,8},{10,11... | collective-permute-start | bytes 393224 | tf_op jit(solution)/shard_map/ppermute | solution.py:450
  72.4 7.2 %copy-start = (bf16[2,16,128,256]{3,2,1,0:T(8,128)(2,1)S(1)}, bf16[2,16,128,256]{3,2,1,0:T(8,128)(2,1)}, u32[]{:S(2)}) copy-start(bf16[2,16,128,256]{3,2,1,0:T(8,128)(2,1)} %state.3) | copy-start | bytes 6291460
